TPU v7x, 256 devices: a whole 4x4x8 slice. The times are simulated.
256 devices in a mesh: dp: 32 (over y, z), tensor: 4 (over x_lo, core), query: 2 (over x_hi).
Axes of the slice: x: 4 (x_hi: 2, x_lo: 2; x = x_hi * 2 + x_lo), y: 4, z: 8, core: 2. Of those that a mesh axis runs over, the one named last changes fastest.
Arguments:
- hidden_acts: bfloat16 [65536, 14336], P(('dp', 'query'), 'tensor'), may hold values from -6 to 6
- out_grads: bfloat16 [65536, 4096], P(('dp', 'query'), 'tensor'), may hold values from -6 to 6
- proj_in: bfloat16 [14336, 64], P('tensor'), may hold values from -0.046875 to 0.046875
- proj_out: bfloat16 [4096, 64], P('tensor'), may hold values from -0.09375 to 0.09375
- queries: bfloat16 [2048, 4096], P('query', 'dp'), may hold values from -1.5 to 1.5
- owner: int32 [256], P('dp'), may hold values from 0 to 31
Outputs:
- scores: float32 [256, 2048], P('dp', 'query')
- owner_totals: float32 [32, 2048], P('dp', 'query')
Inputs may be any that keep to these rules, and one draw needn't show every extreme that they name: owner index of each example.
All inputs are finite; a program needn't handle non-finite values.
Results may differ from a plain program's by a relative error of at most 0.005.
Values may be sent and summed in bfloat16 or wider, within the bound.
A program may use at most 64 MiB of HBM per device.

v0:
```python
import jax
import jax.numpy as jnp
from jax import lax
from jax.sharding import PartitionSpec as P

TOK = 256
OWN_DEV = 1


def make_sketches(projected, sketch_rank):
    examples_here = projected.shape[0] // TOK
    left_side = (
        projected[:, :sketch_rank].astype(jnp.bfloat16).reshape(examples_here, TOK, sketch_rank)
    )
    right_side = (
        projected[:, sketch_rank:].astype(jnp.bfloat16).reshape(examples_here, TOK, sketch_rank)
    )
    outer = (
        jnp.einsum("eti,etj->eij", left_side, right_side, preferred_element_type=jnp.float32) / TOK
    )
    return outer.reshape(examples_here, sketch_rank * sketch_rank).astype(jnp.bfloat16)


def shards(hidden_acts, out_grads, proj_in, proj_out, queries, owner):
    sketch_rank = proj_in.shape[1]
    joined = lax.psum(
        jnp.concatenate(
            [
                jnp.dot(hidden_acts, proj_in, preferred_element_type=jnp.float32),
                jnp.dot(out_grads, proj_out, preferred_element_type=jnp.float32),
            ],
            axis=1,
        ),
        "tensor",
    )
    sketches = make_sketches(joined, sketch_rank)
    paired = lax.all_gather(sketches, "query", axis=0, tiled=True)
    scores = lax.dot_general(
        paired,
        lax.all_gather(queries, "dp", axis=1, tiled=True),
        (((1,), (1,)), ((), ())),
        preferred_element_type=jnp.float32,
    )
    owner_count = lax.axis_size("dp") * OWN_DEV
    owner_onehot = (owner[:, None] == jnp.arange(owner_count, dtype=jnp.int32)[None, :]).astype(
        jnp.float32
    )
    owner_partial = jnp.dot(owner_onehot.T, scores, precision=lax.Precision.HIGHEST)
    owner_totals = lax.psum_scatter(owner_partial, "dp", scatter_dimension=0, tiled=True)
    return (scores, owner_totals)


def solution(mesh):
    in_specs = (
        P(("dp", "query"), "tensor"),
        P(("dp", "query"), "tensor"),
        P("tensor", None),
        P("tensor", None),
        P("query", "dp"),
        P("dp"),
    )
    out_specs = (P("dp", "query"), P("dp", "query"))
    return jax.shard_map(shards, mesh=mesh, in_specs=in_specs, out_specs=out_specs, check_vma=False)
```

profile of v0, /device:TPU:1, one launch (start us, length us, event | category | flops | bytes accessed | tf_op | source)
XLA Modules:
  0.0 268.2 jit_solution(11541431354758214179)
XLA Ops:
  7.2 0.0 copy-start
  7.2 0.0 all-gather.3.cloned.1.call-start
  7.2 0.7 all-gather.3.cloned.1.call-update
  7.9 0.0 all-reduce.4.cloned.1.call-start
  8.0 0.8 copy-done
  8.8 1.7 fusion.9
  10.4 5.5 %fusion.8 = f32[1024,64]{0,1:T(8,128)S(1)} fusion(bf16[1024,3584]{1,0:T(8,128)(2,1)} %param.6, bf16[3584,64]{0,1:T(8,128)(2,1)} %param.8), kind=kOutput, calls=%fused_computation.12 | convolution fusion | flops 469762048 | bytes 8060928 | tf_op jit(solution)/shard_map/dot_general | solution.py:29
  15.9 0.0 copy-start.2
  15.9 0.0 copy-start.3
  16.0 17.8 %all-reduce.5 = bf16[1024,128]{0,1:T(8,128)(2,1)S(1)} all-reduce(f32[1024,128]{0,1:T(8,128)S(1)} %pad_maximum_fusion), channel_id=1, replica_groups=mesh['dp'=32,'tensor'=4,'query'=2] {'tensor'}, use_global_device_ids=true, to_apply=%region_0.0 | all-reduce | flops 131072 | bytes 786432 | tf_op jit(solution)/shard_map/psum | solution.py:26
  33.8 0.2 fusion
  34.0 0.1 reshape.15
  34.1 4.9 %all-gather = bf16[2,4,4096]{2,1,0:T(4,128)(2,1)S(1)} all-gather(bf16[1,4,4096]{2,1,0:T(4,128)(2,1)S(1)} %reshape.15), channel_id=1, replica_groups=mesh['dp'=32,'tensor'=4,'query'=2] {'query'}, dimensions={0}, use_global_device_ids=true | all-gather | bytes 98304 | tf_op jit(solution)/shard_map/all_gather | solution.py:37
  39.1 76.5 %all-gather.3.cloned.1.call-done = bf16[1024,4096]{1,0:T(8,128)(2,1)} async-done(((bf16[1024,128]{1,0:T(8,128)(2,1)}), bf16[1024,4096]{1,0:T(8,128)(2,1)}) %all-gather.3.cloned.1.call-update) | async-done | bytes 8388624 | tf_op jit(solution)/shard_map/all_gather | solution.py:40
  115.5 5.6 %fusion.10 = f32[8,1024]{1,0:T(8,128)S(1)} fusion(bf16[8,4096]{1,0:T(8,128)(2,1)S(1)} %reshape.16, bf16[1024,4096]{1,0:T(8,128)(2,1)} %all-gather.3.cloned.1.call-done), kind=kOutput, calls=%fused_computation.14 | convolution fusion | flops 67108864 | bytes 8486912 | tf_op jit(solution)/shard_map/dot_general | solution.py:38
  121.2 0.0 copy-done.2
  121.2 0.0 copy-start.1
  121.2 1.0 fusion.5
  122.2 0.0 all-reduce.4.cloned.1.call-update
  122.2 0.0 copy-done.3
  122.2 0.6 dynamic-slice
  122.8 136.6 %all-reduce.4.cloned.1.call-done = f32[32,1024]{1,0:T(8,128)} async-done(((f32[32,1024]{1,0:T(8,128)}), f32[32,1024]{1,0:T(8,128)}) %all-reduce.4.cloned.1.call-update) | async-done | bytes 131088
  259.4 2.0 constant_dynamic-slice_fusion
  261.4 0.0 copy-done.1
  (3 shorter events, 0.1 us)
Async XLA Ops:
  7.2 1.6 copy-start
  7.2 108.4 %all-gather.3.cloned.1.call-start = ((), (), s32[]{:S(2)}) async-start(), calls=%async_computation | async-start | bytes 8650752 | tf_op jit(solution)/shard_map/all_gather | solution.py:40
  7.9 251.5 %all-reduce.4.cloned.1.call-start = ((), (), s32[]{:S(2)}) async-start(), calls=%async_computation.1 | async-start | bytes 262144
  15.9 105.3 %copy-start.2 = (s32[8]{0:T(128)S(1)}, s32[8]{0:T(128)}, u32[]{:S(2)}) copy-start(s32[8]{0:T(128)} %param.11) | copy-start | bytes 100
  15.9 106.3 %copy-start.3 = (u32[256]{0:T(256)S(1)}, u32[256]{0:T(256)}, u32[]{:S(2)}) copy-start(u32[256]{0:T(256)} %constant.6) | copy-start | bytes 3076
  121.2 140.2 %copy-start.1 = (f32[8,1024]{1,0:T(8,128)}, f32[8,1024]{1,0:T(8,128)S(1)}, u32[]{:S(2)}) copy-start(f32[8,1024]{1,0:T(8,128)S(1)} %fusion.10) | copy-start | bytes 98308
Sparse Core Ops, SparseCore 0:
  10.5 105.0 all-gather.2
  122.3 137.0 all-reduce.3
where the time goes:
time: 271 us; the launch traced here: 268 us
  waiting for transfers between devices  214 us (79%)
  blocking collectives  22.8 us (8%)
  between operations  14.1 us (5%)
  matrix products  13.9 us (5%)
  local copies, waits for them, and re-layouts  3.56 us (1%)
    unnamed x3, waiting for transfers between devices  137 us
    all_gather x1, waiting for transfers between devices, shards(): lax.all_gather(queries, 'dp', axis=1, tiled=True)  76.5 us
    psum x1, blocking collectives, shards(): lax.psum(jnp.concatenate([jnp.dot(hidden_acts, proj_in, preferred_element...  17.8 us
    dot_general x1, matrix products, shards(): lax.dot_general(paired, lax.all_gather(queries, 'dp', axis=1, tiled=True)...  5.64 us
    dot_general x1, matrix products, shards(): jnp.dot(hidden_acts, proj_in, preferred_element_type=jnp.float32)  5.46 us
  transfers between devices with their start and end apart: 2, of which 2 were waited for; matrix products, arithmetic and copies ran while one was open for 3% of the time, Pallas kernels for 0%

commit v1 on v0

v1 whole, which is shorter than its diff:
```python
import functools

import jax
import jax.numpy as jnp
from jax import lax
from jax.experimental import pallas as pl
from jax.experimental.pallas import tpu as pltpu
from jax.sharding import PartitionSpec as P

MESH = pl.DeviceIdType.MESH
NT = (((1,), (1,)), ((), ()))
TN = (((0,), (0,)), ((), ()))

RANK = 64
TOK = 256
NY, NZ = 4, 8
NT_DEV = 4
LINE = 8
NA, NB = 8, 4
QS = 256
CHUNK = 128
AHEAD = 3
F32, BF16 = jnp.float32, jnp.bfloat16


def dp_of(a, b):
    return b * NZ + a


def kernel(
    h_ref, g_ref, wi_ref, wo_ref, q_ref, owner_ref,
    scores_ref, totals_ref,
    hv, gv, wiv, wov, cross, mate, own, cross_in, mate_in,
    outer, sketch, land, qv, owner_s, owner_t, owner_in,
    part, opart, part_in, opart_in, sc, oo, sc_in, oo_in,
    load_sem, w_sem, misc_sem, rs_send, rs_recv, q_send, q_recv, ow_send, ow_recv,
    s1_send, s1_recv, s2_send, s2_recv, s3_send, s3_recv,
):
    dp, t, hq = lax.axis_index("dp"), lax.axis_index("tensor"), lax.axis_index("query")
    a, b = dp % NZ, dp // NZ
    m = hq * NT_DEV + t
    e_here = a * LINE + m

    far = (t + 2) % NT_DEV
    blocks = (far, far + 1 - 2 * (far % 2), t + 1 - 2 * (t % 2), t)

    def load(c):
        rows = pl.ds(pl.multiple_of(blocks[c // 2] * TOK + (c % 2) * CHUNK, CHUNK), CHUNK)
        return (
            pltpu.make_async_copy(h_ref.at[rows], hv.at[c], load_sem.at[0, c]),
            pltpu.make_async_copy(g_ref.at[rows], gv.at[c], load_sem.at[1, c]),
        )

    chunks = len(blocks) * TOK // CHUNK
    loads = [load(c) for c in range(chunks)]
    w_in = pltpu.make_async_copy(wi_ref, wiv, w_sem.at[0])
    w_out = pltpu.make_async_copy(wo_ref, wov, w_sem.at[1])
    w_in.start()
    loads[0][0].start()
    w_out.start()
    loads[0][1].start()
    for c in range(1, AHEAD):
        for copy in loads[c]:
            copy.start()
    q_rows = pl.ds(pl.multiple_of(t * QS, QS), QS)
    q_own = pltpu.make_async_copy(q_ref.at[q_rows], qv.at[b], misc_sem.at[0])
    o_own = pltpu.make_async_copy(owner_ref, owner_s, misc_sem.at[1])
    q_own.start()
    o_own.start()

    def in_plane(i):
        s = (e_here + i) % (NA * LINE)
        return {"dp": dp_of(s // LINE, b), "tensor": s % NT_DEV, "query": s % LINE // NT_DEV}, s

    def along_b(i):
        s = (b * NT_DEV + t + i) % (NB * NT_DEV)
        return {"dp": dp_of(a, s // NT_DEV), "tensor": s % NT_DEV}, s

    barrier = pltpu.get_barrier_semaphore()

    def greet_plane(i, _):
        pl.semaphore_signal(barrier, inc=1, device_id=in_plane(i)[0], device_id_type=MESH)
        return _

    def greet_b(i, _):
        to = {"dp": dp_of(a, (b + 1 + i // NT_DEV) % NB), "tensor": i % NT_DEV}
        pl.semaphore_signal(barrier, inc=1, device_id=to, device_id_type=MESH)
        return _

    lax.fori_loop(1, NA * LINE, greet_plane, 0)
    lax.fori_loop(0, (NB - 1) * NT_DEV, greet_b, 0)

    rs = []
    for c in range(chunks):
        if c + AHEAD < chunks:
            for copy in loads[c + AHEAD]:
                copy.start()
        if c == 0:
            w_in.wait()
        loads[c][0].wait()
        left = lax.dot_general(hv[c], wiv[...], NT, preferred_element_type=F32)
        if c == 0:
            w_out.wait()
        loads[c][1].wait()
        right = lax.dot_general(gv[c], wov[...], NT, preferred_element_type=F32)
        both = jnp.concatenate([left, right], axis=1)
        rows = pl.ds(c % 2 * CHUNK, CHUNK)
        if c < 4:
            cross[c // 2, rows, :] = both.astype(BF16)
        elif c < 6:
            mate[rows, :] = both
        else:
            own[rows, :] = both
        if c == 5:
            pl.semaphore_wait(barrier, NA * LINE - 1 + (NB - 1) * NT_DEV)
            for i in range(3):
                rs.append(
                    pltpu.make_async_remote_copy(
                        src_ref=cross.at[i] if i < 2 else mate,
                        dst_ref=cross_in.at[i] if i < 2 else mate_in,
                        send_sem=rs_send.at[i],
                        recv_sem=rs_recv.at[i],
                        device_id={"tensor": blocks[i]},
                        device_id_type=MESH,
                    )
                )
                rs[-1].start()

    q_own.wait()

    def send_q(i, _):
        pltpu.make_async_remote_copy(
            src_ref=q_ref.at[
                pl.ds(pl.multiple_of(t * QS, QS), QS)
            ],
            dst_ref=qv.at[b],
            send_sem=q_send,
            recv_sem=q_recv,
            device_id={"dp": dp_of(a, (b + i) % NB)},
            device_id_type=MESH,
        ).start()
        return _

    lax.fori_loop(1, NB, send_q, 0)
    o_own.wait()
    row = lax.broadcasted_iota(jnp.int32, (8, 128), 0)
    tile = jnp.zeros((8, 128), jnp.int32)
    for e in range(8):
        tile = jnp.where(row == e, owner_s[e], tile)
    owner_t[...] = tile
    owner_in[a] = tile

    def send_owner(i, _):
        pltpu.make_async_remote_copy(
            src_ref=owner_t,
            dst_ref=owner_in.at[a],
            send_sem=ow_send,
            recv_sem=ow_recv,
            device_id={"dp": dp_of((a + i) % NA, b)},
            device_id_type=MESH,
        ).start()
        return _

    lax.fori_loop(1, NA, send_owner, 0)

    for copy in rs:
        copy.wait_recv()
    whole = (
        own[...] + mate_in[...] + cross_in[0].astype(F32) + cross_in[1].astype(F32)
    ).astype(BF16)
    outer[...] = lax.dot_general(whole, whole, TN, preferred_element_type=F32) * (1.0 / TOK)
    lane = lax.broadcasted_iota(jnp.int32, (NB, 128), 1)
    for i in range(NA):
        even = outer[pl.ds(2 * i, NB, stride=2 * NZ), :]
        odd = outer[pl.ds(2 * i + 1, NB, stride=2 * NZ), :]
        sketch[i] = jnp.where(lane < RANK, pltpu.roll(even, RANK, 1), odd)
    land[e_here] = sketch[a]

    def send_sketch(i, _):
        to, s = in_plane(i)
        pltpu.make_async_remote_copy(
            src_ref=sketch.at[s // LINE],
            dst_ref=land.at[e_here],
            send_sem=s1_send,
            recv_sem=s1_recv,
            device_id=to,
            device_id_type=MESH,
        ).start()
        return _

    lax.fori_loop(1, NA * LINE, send_sketch, 0)

    def settle(ref, sem):
        pltpu.make_async_copy(ref, ref, sem).wait()

    settle(qv.at[pl.ds(0, NB - 1)], q_recv)
    settle(owner_in.at[pl.ds(0, NA - 1)], ow_recv)
    settle(land.at[pl.ds(0, NA * LINE - 1)], s1_recv)

    total = jnp.zeros((NA * LINE, QS), F32)
    for i in range(NB):
        total += lax.dot_general(
            land[:, i, :].astype(BF16), qv[i], NT, preferred_element_type=F32
        )
    part[...] = total.reshape(NA, 8, QS)
    lanes = lax.broadcasted_iota(jnp.int32, (NA * LINE, 128), 1)
    named = dp_of(lanes // NB, lanes % NB)
    onehot = (owner_in[...].reshape(NA * LINE, 128) == named).astype(F32)
    summed = lax.dot_general(
        onehot, total, TN, precision=lax.Precision.HIGHEST, preferred_element_type=F32
    )
    for i in range(NA):
        opart[i] = summed[i * NB : (i + 1) * NB]
    part_in[a] = part[a]
    opart_in[a] = opart[a]

    def send_part(i, _):
        s = (a + i) % NA
        for src, dst, k in ((part, part_in, 0), (opart, opart_in, 1)):
            pltpu.make_async_remote_copy(
                src_ref=src.at[s],
                dst_ref=dst.at[a],
                send_sem=s2_send.at[k],
                recv_sem=s2_recv.at[k],
                device_id={"dp": dp_of(s, b)},
                device_id_type=MESH,
            ).start()
        return _

    lax.fori_loop(1, NA, send_part, 0)
    settle(part_in.at[pl.ds(0, NA - 1)], s2_recv.at[0])
    settle(opart_in.at[pl.ds(0, NA - 1)], s2_recv.at[1])
    sc[...] = jnp.sum(part_in[...], axis=0)
    owned = jnp.sum(opart_in[...], axis=0)
    for i in range(NB):
        oo[i] = owned[i : i + 1]

    sc_in[t] = sc[...]
    oo_in[b * NT_DEV + t] = oo[b]

    def send_total(i, _):
        to, s = along_b(i)
        pltpu.make_async_remote_copy(
            src_ref=oo.at[s // NT_DEV],
            dst_ref=oo_in.at[b * NT_DEV + t],
            send_sem=s3_send.at[1],
            recv_sem=s3_recv.at[1],
            device_id=to,
            device_id_type=MESH,
        ).start()
        return _

    def send_scores(i, _):
        pltpu.make_async_remote_copy(
            src_ref=sc,
            dst_ref=sc_in.at[t],
            send_sem=s3_send.at[0],
            recv_sem=s3_recv.at[0],
            device_id={"tensor": (t + i) % NT_DEV},
            device_id_type=MESH,
        ).start()
        return _

    lax.fori_loop(1, NB * NT_DEV, send_total, 0)
    lax.fori_loop(1, NT_DEV, send_scores, 0)
    settle(sc_in.at[pl.ds(0, NT_DEV - 1)], s3_recv.at[0])
    for i in range(NT_DEV):
        scores_ref[:, i * QS : (i + 1) * QS] = sc_in[i]
    settle(oo_in.at[pl.ds(0, NB * NT_DEV - 1)], s3_recv.at[1])
    for i in range(NT_DEV):
        row = oo_in[i]
        for j in range(1, NB):
            row = row + oo_in[j * NT_DEV + i]
        totals_ref[:, i * QS : (i + 1) * QS] = row

    for copy in rs:
        copy.wait_send()
    settle(qv.at[pl.ds(0, NB - 1)], q_send)
    settle(owner_in.at[pl.ds(0, NA - 1)], ow_send)
    settle(land.at[pl.ds(0, NA * LINE - 1)], s1_send)
    settle(part_in.at[pl.ds(0, NA - 1)], s2_send.at[0])
    settle(opart_in.at[pl.ds(0, NA - 1)], s2_send.at[1])
    settle(sc_in.at[pl.ds(0, NT_DEV - 1)], s3_send.at[0])
    settle(oo_in.at[pl.ds(0, NB * NT_DEV - 1)], s3_send.at[1])


def shards(hidden_acts, out_grads, proj_in, proj_out, queries, owner):
    ff, d = hidden_acts.shape[1], out_grads.shape[1]
    chunks = hidden_acts.shape[0] // CHUNK
    entries = queries.shape[1]
    any_ = pl.BlockSpec(memory_space=pl.ANY)
    vmem = pl.BlockSpec(memory_space=pltpu.VMEM)
    dma = pltpu.SemaphoreType.DMA
    return pl.pallas_call(
        kernel,
        out_shape=(
            jax.ShapeDtypeStruct((8, NT_DEV * QS), F32),
            jax.ShapeDtypeStruct((1, NT_DEV * QS), F32),
        ),
        in_specs=[any_] * 6,
        out_specs=(vmem, vmem),
        scratch_shapes=[
            pltpu.VMEM((chunks, CHUNK, ff), BF16),
            pltpu.VMEM((chunks, CHUNK, d), BF16),
            pltpu.VMEM((RANK, ff), BF16),
            pltpu.VMEM((RANK, d), BF16),
            pltpu.VMEM((2, TOK, 2 * RANK), BF16),
            pltpu.VMEM((TOK, 2 * RANK), F32),
            pltpu.VMEM((TOK, 2 * RANK), F32),
            pltpu.VMEM((2, TOK, 2 * RANK), BF16),
            pltpu.VMEM((TOK, 2 * RANK), F32),
            pltpu.VMEM((128, 128), F32),
            pltpu.VMEM((NA, NB, 128), F32),
            pltpu.VMEM((NA * LINE, NB, 128), F32),
            pltpu.VMEM((NB, QS, entries), BF16),
            pltpu.SMEM((8,), jnp.int32),
            pltpu.VMEM((8, 128), jnp.int32),
            pltpu.VMEM((NA, 8, 128), jnp.int32),
            pltpu.VMEM((NA, 8, QS), F32),
            pltpu.VMEM((NA, NB, QS), F32),
            pltpu.VMEM((NA, 8, QS), F32),
            pltpu.VMEM((NA, NB, QS), F32),
            pltpu.VMEM((8, QS), F32),
            pltpu.VMEM((NB, 1, QS), F32),
            pltpu.VMEM((NT_DEV, 8, QS), F32),
            pltpu.VMEM((NB * NT_DEV, 1, QS), F32),
            dma((2, chunks)),
            dma((2,)),
            dma((2,)),
            dma((3,)),
            dma((3,)),
            dma,
            dma,
            dma,
            dma,
            dma,
            dma,
            dma((2,)),
            dma((2,)),
            dma((2,)),
            dma((2,)),
        ],
        compiler_params=pltpu.CompilerParams(
            collective_id=0, has_side_effects=True, vmem_limit_bytes=63 << 20
        ),
        name="attribution",
    )(hidden_acts, out_grads, proj_in.T, proj_out.T, queries, owner)


def solution(mesh):
    in_specs = (
        P(("dp", "query"), "tensor"),
        P(("dp", "query"), "tensor"),
        P("tensor", None),
        P("tensor", None),
        P("query", "dp"),
        P("dp"),
    )
    out_specs = (P("dp", "query"), P("dp", "query"))
    return jax.shard_map(shards, mesh=mesh, in_specs=in_specs, out_specs=out_specs, check_vma=False)
```

time: 271 us -> 41.5 us (0.15)
  waiting for transfers between devices: 214 us -> 0 us
  Pallas kernels: 0 us -> 38 us
  blocking collectives: 22.8 us -> 0 us
  matrix products: 13.9 us -> 0 us
  between operations: 14.1 us -> 0.64 us
    unnamed x3 -> x0, waiting for transfers between devices: 137 us -> none
    all_gather x1 -> x0, waiting for transfers between devices: 76.5 us -> none  [shards(): lax.all_gather(queries, 'dp', axis=1, tiled=True)]
    pallas_call x0 -> x1, Pallas kernels: none -> 38 us  [shards(): pl.pallas_call(kernel, out_shape=(jax.ShapeDtypeStruct((8, NT_DEV * QS),...]
    psum x1 -> x0, blocking collectives: 17.8 us -> none  [shards(): lax.psum(jnp.concatenate([jnp.dot(hidden_acts, proj_in, preferred_element...]
    dot_general x5 -> x0, matrix products: 13.9 us -> none  [the longest x1 5.64 us: shards(): lax.dot_general(paired, lax.all_gather(queries, 'dp', axis=1, tiled=True)...]
    all_gather x1 -> x0, blocking collectives: 4.95 us -> none  [shards(): paired = lax.all_gather(sketches, 'query', axis=0, tiled=True)]
  transfers between devices with their start and end apart: 2 -> 0, of which waited for: 2 -> 0; matrix products, arithmetic and copies ran while one was open for 3% -> 0% of each run, Pallas kernels for 0% -> 0%
where the time goes in v1:
time: 41.5 us; the launch traced here: 41.3 us
  Pallas kernels  38 us (92%)
  local copies, waits for them, and re-layouts  2.65 us (6%)
  between operations  0.64 us (2%)
    pallas_call x1, Pallas kernels, shards(): pl.pallas_call(kernel, out_shape=(jax.ShapeDtypeStruct((8, NT_DEV * QS),...  38 us
    unnamed x2, local copies, waits for them, and re-layouts  2.65 us

profile of v1, /device:TPU:1, one launch (start us, length us, event | category | flops | bytes accessed | tf_op | source)
XLA Modules:
  0.0 41.3 jit_solution(15065727131374582343)
XLA Ops:
  0.6 38.0 %attribution.1 = (f32[8,1024]{1,0:T(8,128)}, f32[1,1024]{1,0:T(1,128)}) custom-call(bf16[1024,3584]{1,0:T(8,128)(2,1)} %h_ref.1, bf16[1024,1024]{1,0:T(8,128)(2,1)} %g_ref.1, bf16[64,3584]{1,0:T(8,128)(2,1)} %bitcast.2, bf16[64,1024]{1,0:T(8,128)(2,1)} %bitcast.3, bf16[1024,128]{1,0:T(8,128)(2,1)} %q_ref.1, s32[8]{0:T(128)} %owner_ref.1), custom_call_target="tpu_custom_call" | custom-call | tf_op jit(solution)/shard_map/attribution/pallas_call | solution.py:294
  38.7 1.4 %copy.10 = f32[8,1024]{1,0:T(8,128)} copy(f32[8,1024]{1,0:T(8,128)} %get-tuple-element.4) | data formatting | bytes 65536
  40.0 1.3 %copy.11 = f32[1,1024]{1,0:T(1,128)} copy(f32[1,1024]{1,0:T(1,128)} %get-tuple-element.5) | data formatting | bytes 8192

commit v2 on v1

v2 whole, which is shorter than its diff:
```python
import itertools

import jax
import jax.numpy as jnp
from jax import lax
from jax.experimental import pallas as pl
from jax.experimental.pallas import tpu as pltpu
from jax.sharding import PartitionSpec as P

MESH = pl.DeviceIdType.MESH
NT = (((1,), (1,)), ((), ()))
TN = (((0,), (0,)), ((), ()))

RANK = 64
TOK = 256
NY, NZ = 4, 8
NT_DEV = 4
LINE = 8
NA, NB = NY, NZ
NX = 4
QS = 256
CHUNK = 256
PIECES = TOK // CHUNK
AHEAD = 2
F32, BF16 = jnp.float32, jnp.bfloat16


def dp_of(a, b):
    return a * NB + b


def ring(n):
    return sorted(range(n), key=lambda i: -min(i, n - i))


def kernel(
    h_ref, g_ref, wi_ref, wo_ref, q_ref, owner_ref,
    scores_ref, totals_ref,
    hv, gv, wiv, wov, cross, mate, own, cross_in, mate_in,
    outer, sketch, land, qv, owner_s, owner_t, owner_in,
    part, opart, part_in, opart_in, sc, oo, sc_in, oo_in,
    load_sem, w_sem, misc_sem, rs_send, rs_recv, q_send, q_recv, ow_send, ow_recv,
    s1_send, s1_recv, s2_send, s2_recv, s3_send, s3_recv,
):
    dp, t, hq = lax.axis_index("dp"), lax.axis_index("tensor"), lax.axis_index("query")
    a, b = dp // NB, dp % NB
    x, core = hq * 2 + t // 2, t % 2
    m = hq * NT_DEV + t
    e_here = a * LINE + m

    far = (t + 2) % NT_DEV
    blocks = (far, far + 1 - 2 * (far % 2), t + 1 - 2 * (t % 2), t)

    def load(c):
        start = blocks[c // PIECES] * TOK + c % PIECES * CHUNK
        rows = pl.ds(pl.multiple_of(start, CHUNK), CHUNK)
        return (
            pltpu.make_async_copy(h_ref.at[rows], hv.at[c], load_sem.at[0, c]),
            pltpu.make_async_copy(g_ref.at[rows], gv.at[c], load_sem.at[1, c]),
        )

    loads = [load(c) for c in range(NT_DEV * PIECES)]
    w_in = pltpu.make_async_copy(wi_ref, wiv, w_sem.at[0])
    w_out = pltpu.make_async_copy(wo_ref, wov, w_sem.at[1])
    q_rows = pl.ds(pl.multiple_of(t * QS, QS), QS)
    q_own = pltpu.make_async_copy(q_ref.at[q_rows], qv.at[b], misc_sem.at[0])
    o_own = pltpu.make_async_copy(owner_ref, owner_s, misc_sem.at[1])

    a_at = [(a + i) % NA for i in range(NA)]
    b_at = [(b + i) % NB for i in range(NB)]
    x_at = [(x + i) % NX for i in range(NX)]
    lo_at = [(t // 2 + i) % 2 for i in range(2)]
    core_at = [core, 1 - core]
    plane = [
        (a_at[i], x_at[j] % 2 * 2 + core_at[k], x_at[j] // 2)
        for i, j, k in sorted(
            itertools.product(range(NA), range(NX), range(2)),
            key=lambda v: -(min(v[0], NA - v[0]) + min(v[1], NX - v[1])),
        )
        if (i, j, k) != (0, 0, 0)
    ]
    column = [
        (b_at[i], lo_at[j] * 2 + core_at[k])
        for i, j, k in itertools.product(ring(NB), range(1, -1, -1), range(2))
        if (i, j, k) != (0, 0, 0)
    ]
    beyond = column[: -(NT_DEV - 1)]

    barrier = pltpu.get_barrier_semaphore()

    greeted = [{"tensor": j, "query": k} for i, j, k in plane if i is a_at[0]]
    greeted += [{"dp": dp_of(i, b)} for i in a_at[1:]]
    greeted += [{"dp": dp_of(a, b_at[i])} for i in (2, NB - 2, 1, NB - 1)]

    def greet(some):
        for to in some:
            pl.semaphore_signal(barrier, inc=1, device_id=to, device_id_type=MESH)

    w_in.start()
    loads[0][0].start()
    w_out.start()
    loads[0][1].start()
    for c in range(1, AHEAD):
        greet(greeted[c - 1 :: AHEAD - 1])
        for copy in loads[c]:
            copy.start()
    o_own.start()
    q_own.start()

    def queries_to(step, source, i):
        return pltpu.make_async_remote_copy(
            src_ref=qv.at[source],
            dst_ref=qv.at[source],
            send_sem=q_send,
            recv_sem=q_recv.at[step],
            device_id={"dp": dp_of(a, b_at[i])},
            device_id_type=MESH,
        )

    def queries_to(step, source, i):
        return pltpu.make_async_remote_copy(
            src_ref=qv.at[source],
            dst_ref=qv.at[source],
            send_sem=q_send,
            recv_sem=q_recv.at[step],
            device_id={"dp": dp_of(a, b_at[i])},
            device_id_type=MESH,
        )

    rs = []
    for c in range(NT_DEV * PIECES):
        if c == 0:
            w_in.wait()
        loads[c][0].wait()
        left = lax.dot_general(hv[c], wiv[...], NT, preferred_element_type=F32)
        if c == 0:
            w_out.wait()
        loads[c][1].wait()
        if c + AHEAD < NT_DEV * PIECES:
            for copy in loads[c + AHEAD]:
                copy.start()
        right = lax.dot_general(gv[c], wov[...], NT, preferred_element_type=F32)
        both = jnp.concatenate([left, right], axis=1)
        i, rows = c // PIECES, pl.ds(c % PIECES * CHUNK, CHUNK)
        if i < 2:
            cross[i, rows, :] = both.astype(BF16)
        elif i == 2:
            mate[rows, :] = both
        else:
            own[rows, :] = both
        if c % PIECES < PIECES - 1 or i == 3:
            continue
        if i == 0:
            pl.semaphore_wait(barrier, len(greeted))
        rs.append(
            pltpu.make_async_remote_copy(
                src_ref=cross.at[i] if i < 2 else mate,
                dst_ref=cross_in.at[i] if i < 2 else mate_in,
                send_sem=rs_send.at[i],
                recv_sem=rs_recv.at[i],
                device_id={"tensor": blocks[i]},
                device_id_type=MESH,
            )
        )
        rs[-1].start()
        if i == 0:
            o_own.wait()
            row = lax.broadcasted_iota(jnp.int32, (8, 128), 0)
            tile = jnp.zeros((8, 128), jnp.int32)
            for e in range(8):
                tile = jnp.where(row == e, owner_s[e], tile)
            owner_t[...] = tile
            owner_in[a] = tile
            for to in a_at[1:]:
                pltpu.make_async_remote_copy(
                    src_ref=owner_t,
                    dst_ref=owner_in.at[a],
                    send_sem=ow_send,
                    recv_sem=ow_recv,
                    device_id={"dp": dp_of(to, b)},
                    device_id_type=MESH,
                ).start()
        if i == 0:
            q_own.wait()
            for step, j in enumerate((2, NB - 2, 1, NB - 1)):
                queries_to(step, b, j).start()

    def settle(ref, sem):
        pltpu.make_async_copy(ref, ref, sem).wait()

    for copy in rs:
        copy.wait_recv()
    whole = (
        own[...] + mate_in[...] + cross_in[0].astype(F32) + cross_in[1].astype(F32)
    ).astype(BF16)
    outer[...] = lax.dot_general(whole, whole, TN, preferred_element_type=F32) * (1.0 / TOK)
    lane = lax.broadcasted_iota(jnp.int32, (NB, 128), 1)
    for i in range(NA):
        even = outer[pl.ds(2 * i * NB, NB, stride=2), :]
        odd = outer[pl.ds(2 * i * NB + 1, NB, stride=2), :]
        sketch[i] = jnp.where(lane < RANK, pltpu.roll(even, RANK, 1), odd)
    settle(owner_in.at[pl.ds(0, NA - 1)], ow_recv)
    land[e_here] = sketch[a]

    for i, j, k in plane:
        pltpu.make_async_remote_copy(
            src_ref=sketch.at[i],
            dst_ref=land.at[e_here],
            send_sem=s1_send,
            recv_sem=s1_recv,
            device_id={"dp": dp_of(i, b), "tensor": j, "query": k},
            device_id_type=MESH,
        ).start()

    settle(qv.at[0], q_recv.at[0])
    queries_to(4, b_at[NB - 2], 1).start()
    queries_to(5, b_at[NB - 2], 2).start()
    settle(qv.at[0], q_recv.at[1])
    queries_to(6, b_at[2], NB - 1).start()
    settle(land.at[pl.ds(0, NA * LINE - 1)], s1_recv)
    for step in range(2, NB - 1):
        settle(qv.at[0], q_recv.at[step])

    total = jnp.zeros((NA * LINE, QS), F32)
    for i in range(NB):
        total += lax.dot_general(
            land[:, i, :].astype(BF16), qv[i], NT, preferred_element_type=F32
        )
    part[...] = total.reshape(NA, 8, QS)
    lanes = lax.broadcasted_iota(jnp.int32, (NA * LINE, 128), 1)
    named = dp_of(lanes // NB, lanes % NB)
    onehot = (owner_in[...].reshape(NA * LINE, 128) == named).astype(F32)
    summed = lax.dot_general(
        onehot, total, TN, precision=lax.Precision.HIGHEST, preferred_element_type=F32
    )
    for i in range(NA):
        opart[i] = summed[i * NB : (i + 1) * NB]
    part_in[a] = part[a]
    opart_in[a] = opart[a]

    for i in a_at[2:] + a_at[1:2]:
        for src, dst, k in ((part, part_in, 0), (opart, opart_in, 1)):
            pltpu.make_async_remote_copy(
                src_ref=src.at[i],
                dst_ref=dst.at[a],
                send_sem=s2_send.at[k],
                recv_sem=s2_recv.at[k],
                device_id={"dp": dp_of(i, b)},
                device_id_type=MESH,
            ).start()

    settle(part_in.at[pl.ds(0, NA - 1)], s2_recv.at[0])
    settle(opart_in.at[pl.ds(0, NA - 1)], s2_recv.at[1])
    sc[...] = jnp.sum(part_in[...], axis=0)
    owned = jnp.sum(opart_in[...], axis=0)
    for i in range(NB):
        oo[i] = owned[i : i + 1]

    sc_in[t] = sc[...]
    oo_in[b * NT_DEV + t] = oo[b]

    def send_total(i, j):
        pltpu.make_async_remote_copy(
            src_ref=oo.at[i],
            dst_ref=oo_in.at[b * NT_DEV + t],
            send_sem=s3_send.at[1],
            recv_sem=s3_recv.at[1],
            device_id={"dp": dp_of(a, i), "tensor": j},
            device_id_type=MESH,
        ).start()

    for i, j in beyond:
        send_total(i, j)
    for i, j in column[len(beyond) :]:
        pltpu.make_async_remote_copy(
            src_ref=sc,
            dst_ref=sc_in.at[t],
            send_sem=s3_send.at[0],
            recv_sem=s3_recv.at[0],
            device_id={"tensor": j},
            device_id_type=MESH,
        ).start()
        send_total(i, j)
    settle(sc_in.at[pl.ds(0, NT_DEV - 1)], s3_recv.at[0])
    for i in range(NT_DEV):
        scores_ref[:, i * QS : (i + 1) * QS] = sc_in[i]
    settle(oo_in.at[pl.ds(0, NB * NT_DEV - 1)], s3_recv.at[1])
    for i in range(NT_DEV):
        row = oo_in[i]
        for j in range(1, NB):
            row = row + oo_in[j * NT_DEV + i]
        totals_ref[:, i * QS : (i + 1) * QS] = row

    for copy in rs:
        copy.wait_send()
    settle(qv.at[pl.ds(0, NB - 1)], q_send)
    settle(owner_in.at[pl.ds(0, NA - 1)], ow_send)
    settle(land.at[pl.ds(0, NA * LINE - 1)], s1_send)
    settle(part_in.at[pl.ds(0, NA - 1)], s2_send.at[0])
    settle(opart_in.at[pl.ds(0, NA - 1)], s2_send.at[1])
    settle(sc_in.at[pl.ds(0, NT_DEV - 1)], s3_send.at[0])
    settle(oo_in.at[pl.ds(0, NB * NT_DEV - 1)], s3_send.at[1])


def shards(hidden_acts, out_grads, proj_in, proj_out, queries, owner):
    ff, d = hidden_acts.shape[1], out_grads.shape[1]
    pieces = hidden_acts.shape[0] // CHUNK
    entries = queries.shape[1]
    hbm = pl.BlockSpec(memory_space=pl.ANY)
    vmem = pl.BlockSpec(memory_space=pltpu.VMEM)
    dma = pltpu.SemaphoreType.DMA
    return pl.pallas_call(
        kernel,
        out_shape=(
            jax.ShapeDtypeStruct((8, NT_DEV * QS), F32),
            jax.ShapeDtypeStruct((1, NT_DEV * QS), F32),
        ),
        in_specs=[hbm] * 6,
        out_specs=(vmem, vmem),
        scratch_shapes=[
            pltpu.VMEM((pieces, CHUNK, ff), BF16),
            pltpu.VMEM((pieces, CHUNK, d), BF16),
            pltpu.VMEM((RANK, ff), BF16),
            pltpu.VMEM((RANK, d), BF16),
            pltpu.VMEM((2, TOK, 2 * RANK), BF16),
            pltpu.VMEM((TOK, 2 * RANK), F32),
            pltpu.VMEM((TOK, 2 * RANK), F32),
            pltpu.VMEM((2, TOK, 2 * RANK), BF16),
            pltpu.VMEM((TOK, 2 * RANK), F32),
            pltpu.VMEM((128, 128), F32),
            pltpu.VMEM((NA, NB, 128), F32),
            pltpu.VMEM((NA * LINE, NB, 128), F32),
            pltpu.VMEM((NB, QS, entries), BF16),
            pltpu.SMEM((8,), jnp.int32),
            pltpu.VMEM((8, 128), jnp.int32),
            pltpu.VMEM((NA, 8, 128), jnp.int32),
            pltpu.VMEM((NA, 8, QS), F32),
            pltpu.VMEM((NA, NB, QS), F32),
            pltpu.VMEM((NA, 8, QS), F32),
            pltpu.VMEM((NA, NB, QS), F32),
            pltpu.VMEM((8, QS), F32),
            pltpu.VMEM((NB, 1, QS), F32),
            pltpu.VMEM((NT_DEV, 8, QS), F32),
            pltpu.VMEM((NB * NT_DEV, 1, QS), F32),
            dma((2, pieces)),
            dma((2,)),
            dma((2,)),
            dma((3,)),
            dma((3,)),
            dma,
            dma((NB - 1,)),
            dma,
            dma,
            dma,
            dma,
            dma((2,)),
            dma((2,)),
            dma((2,)),
            dma((2,)),
        ],
        compiler_params=pltpu.CompilerParams(
            collective_id=0, has_side_effects=True, vmem_limit_bytes=55168 << 10
        ),
        name="attribution",
    )(hidden_acts, out_grads, proj_in.T, proj_out.T, queries, owner)


def solution(mesh):
    in_specs = (
        P(("dp", "query"), "tensor"),
        P(("dp", "query"), "tensor"),
        P("tensor", None),
        P("tensor", None),
        P("query", "dp"),
        P("dp"),
    )
    out_specs = (P("dp", "query"), P("dp", "query"))
    return jax.shard_map(shards, mesh=mesh, in_specs=in_specs, out_specs=out_specs, check_vma=False)
```

time: 41.5 us -> 33.3 us (0.80)
  Pallas kernels: 38 us -> 30.7 us
  local copies, waits for them, and re-layouts: 2.65 us -> 1.86 us
    pallas_call x1, Pallas kernels: 38 us -> 30.7 us  [shards(): pl.pallas_call(kernel, out_shape=(jax.ShapeDtypeStruct((8, NT_DEV * QS),...]
    unnamed x2 -> x4, local copies, waits for them, and re-layouts: 2.65 us -> 1.86 us
where the time goes in v2:
time: 33.3 us; the launch traced here: 33.2 us
  Pallas kernels  30.7 us (92%)
  local copies, waits for them, and re-layouts  1.86 us (6%)
  between operations  0.65 us (2%)
    pallas_call x1, Pallas kernels, shards(): pl.pallas_call(kernel, out_shape=(jax.ShapeDtypeStruct((8, NT_DEV * QS),...  30.7 us
    unnamed x4, local copies, waits for them, and re-layouts  1.86 us

profile of v2, /device:TPU:1, one launch (start us, length us, event | category | flops | bytes accessed | tf_op | source)
XLA Modules:
  0.0 33.2 jit_solution(2491888221494574195)
XLA Ops:
  0.6 0.0 copy-start
  0.6 0.6 %copy-done = s32[8]{0:T(128)S(1)} copy-done((s32[8]{0:T(128)S(1)}, s32[8]{0:T(128)}, u32[]{:S(2)}) %copy-start) | copy-done | bytes 56
  1.3 30.7 %attribution.1 = (f32[8,1024]{1,0:T(8,128)S(1)}, f32[1,1024]{1,0:T(1,128)S(1)}) custom-call(bf16[1024,3584]{1,0:T(8,128)(2,1)} %h_ref.1, bf16[1024,1024]{1,0:T(8,128)(2,1)} %g_ref.1, bf16[64,3584]{1,0:T(8,128)(2,1)} %bitcast.2, bf16[64,1024]{1,0:T(8,128)(2,1)} %bitcast.3, bf16[1024,128]{1,0:T(8,128)(2,1)} %q_ref.1, s32[8]{0:T(128)S(1)} %copy-done), custom_call_target="tpu_custom_call" | custom-call | tf_op jit(solution)/shard_map/attribution/pallas_call | solution.py:312
  32.0 0.6 %copy.10 = f32[8,1024]{1,0:T(8,128)} copy(f32[8,1024]{1,0:T(8,128)S(1)} %get-tuple-element.4) | data formatting | bytes 65536
  32.6 0.6 %copy.11 = f32[1,1024]{1,0:T(1,128)} copy(f32[1,1024]{1,0:T(1,128)S(1)} %get-tuple-element.5) | data formatting | bytes 8192
Async XLA Ops:
  0.6 0.7 %copy-start = (s32[8]{0:T(128)S(1)}, s32[8]{0:T(128)}, u32[]{:S(2)}) copy-start(s32[8]{0:T(128)} %owner_ref.1) | copy-start | bytes 100

commit v3 on v2

--- a/solution.py
+++ b/solution.py
@@ -19,8 +19,6 @@
 NA, NB = NY, NZ
 NX = 4
 QS = 256
-CHUNK = 256
-PIECES = TOK // CHUNK
 AHEAD = 2
 F32, BF16 = jnp.float32, jnp.bfloat16
 
@@ -52,14 +50,13 @@
     blocks = (far, far + 1 - 2 * (far % 2), t + 1 - 2 * (t % 2), t)
 
     def load(c):
-        start = blocks[c // PIECES] * TOK + c % PIECES * CHUNK
-        rows = pl.ds(pl.multiple_of(start, CHUNK), CHUNK)
+        rows = pl.ds(pl.multiple_of(blocks[c] * TOK, TOK), TOK)
         return (
             pltpu.make_async_copy(h_ref.at[rows], hv.at[c], load_sem.at[0, c]),
             pltpu.make_async_copy(g_ref.at[rows], gv.at[c], load_sem.at[1, c]),
         )
 
-    loads = [load(c) for c in range(NT_DEV * PIECES)]
+    loads = [load(c) for c in range(NT_DEV)]
     w_in = pltpu.make_async_copy(wi_ref, wiv, w_sem.at[0])
     w_out = pltpu.make_async_copy(wo_ref, wov, w_sem.at[1])
     q_rows = pl.ds(pl.multiple_of(t * QS, QS), QS)
@@ -103,9 +100,9 @@
     for c in range(1, AHEAD):
         greet(greeted[c - 1 :: AHEAD - 1])
         for copy in loads[c]:
-            copy.start()
-    o_own.start()
-    q_own.start()
+            copy.start(priority=1)
+    o_own.start(priority=1)
+    q_own.start(priority=1)
 
     def queries_to(step, source, i):
         return pltpu.make_async_remote_copy(
@@ -127,43 +124,54 @@
             device_id_type=MESH,
         )
 
-    rs = []
-    for c in range(NT_DEV * PIECES):
+    rs = [
+        pltpu.make_async_remote_copy(
+            src_ref=cross.at[i] if i < 2 else mate,
+            dst_ref=cross_in.at[i] if i < 2 else mate_in,
+            send_sem=rs_send.at[i],
+            recv_sem=rs_recv.at[i],
+            device_id={"tensor": blocks[i]},
+            device_id_type=MESH,
+        )
+        for i in range(NT_DEV - 1)
+    ]
+
+    def meet(ready):
+        pl.semaphore_wait(barrier, len(greeted))
+        for copy in rs[:ready]:
+            copy.start()
+        for to in a_at[1:]:
+            pltpu.make_async_remote_copy(
+                src_ref=owner_t,
+                dst_ref=owner_in.at[a],
+                send_sem=ow_send,
+                recv_sem=ow_recv,
+                device_id={"dp": dp_of(to, b)},
+                device_id_type=MESH,
+            ).start()
+        for step, j in enumerate((2, NB - 2, 1, NB - 1)):
+            queries_to(step, b, j).start()
+
+    early = b < 1
+    for c in range(NT_DEV):
         if c == 0:
             w_in.wait()
-        loads[c][0].wait()
-        left = lax.dot_general(hv[c], wiv[...], NT, preferred_element_type=F32)
+            w_out.wait()
+        for copy in loads[c]:
+            copy.wait()
+        if c + AHEAD < NT_DEV:
+            for copy in loads[c + AHEAD]:
+                copy.start(priority=1)
+        left = lax.dot_general(wiv[...], hv[c], NT, preferred_element_type=F32)
+        right = lax.dot_general(wov[...], gv[c], NT, preferred_element_type=F32)
+        both = jnp.concatenate([left, right], axis=0)
+        if c < 2:
+            cross[c] = both.astype(BF16)
+        elif c == 2:
+            mate[...] = both
+        else:
+            own[...] = both
         if c == 0:
-            w_out.wait()
-        loads[c][1].wait()
-        if c + AHEAD < NT_DEV * PIECES:
-            for copy in loads[c + AHEAD]:
-                copy.start()
-        right = lax.dot_general(gv[c], wov[...], NT, preferred_element_type=F32)
-        both = jnp.concatenate([left, right], axis=1)
-        i, rows = c // PIECES, pl.ds(c % PIECES * CHUNK, CHUNK)
-        if i < 2:
-            cross[i, rows, :] = both.astype(BF16)
-        elif i == 2:
-            mate[rows, :] = both
-        else:
-            own[rows, :] = both
-        if c % PIECES < PIECES - 1 or i == 3:
-            continue
-        if i == 0:
-            pl.semaphore_wait(barrier, len(greeted))
-        rs.append(
-            pltpu.make_async_remote_copy(
-                src_ref=cross.at[i] if i < 2 else mate,
-                dst_ref=cross_in.at[i] if i < 2 else mate_in,
-                send_sem=rs_send.at[i],
-                recv_sem=rs_recv.at[i],
-                device_id={"tensor": blocks[i]},
-                device_id_type=MESH,
-            )
-        )
-        rs[-1].start()
-        if i == 0:
             o_own.wait()
             row = lax.broadcasted_iota(jnp.int32, (8, 128), 0)
             tile = jnp.zeros((8, 128), jnp.int32)
@@ -171,34 +179,36 @@
                 tile = jnp.where(row == e, owner_s[e], tile)
             owner_t[...] = tile
             owner_in[a] = tile
-            for to in a_at[1:]:
-                pltpu.make_async_remote_copy(
-                    src_ref=owner_t,
-                    dst_ref=owner_in.at[a],
-                    send_sem=ow_send,
-                    recv_sem=ow_recv,
-                    device_id={"dp": dp_of(to, b)},
-                    device_id_type=MESH,
-                ).start()
-        if i == 0:
             q_own.wait()
-            for step, j in enumerate((2, NB - 2, 1, NB - 1)):
-                queries_to(step, b, j).start()
+            pl.when(jnp.logical_not(early))(lambda: meet(1))
+        elif c < 3:
+            pl.when(jnp.logical_not(early))(rs[c].start)
+        else:
+            pl.when(early)(lambda: meet(3))
 
     def settle(ref, sem):
         pltpu.make_async_copy(ref, ref, sem).wait()
+
+    settle(qv.at[0], q_recv.at[0])
+    queries_to(5, b_at[NB - 2], 2).start()
+    queries_to(4, b_at[NB - 2], 1).start()
+    settle(qv.at[0], q_recv.at[1])
+    queries_to(6, b_at[2], NB - 1).start()
 
     for copy in rs:
         copy.wait_recv()
     whole = (
         own[...] + mate_in[...] + cross_in[0].astype(F32) + cross_in[1].astype(F32)
     ).astype(BF16)
-    outer[...] = lax.dot_general(whole, whole, TN, preferred_element_type=F32) * (1.0 / TOK)
+    twice = jnp.concatenate([whole[RANK:], whole[RANK:]], axis=0)
+    outer[...] = lax.dot_general(
+        whole[:RANK], twice, NT, preferred_element_type=F32
+    ) * (1.0 / TOK)
     lane = lax.broadcasted_iota(jnp.int32, (NB, 128), 1)
     for i in range(NA):
         even = outer[pl.ds(2 * i * NB, NB, stride=2), :]
         odd = outer[pl.ds(2 * i * NB + 1, NB, stride=2), :]
-        sketch[i] = jnp.where(lane < RANK, pltpu.roll(even, RANK, 1), odd)
+        sketch[i] = jnp.where(lane < RANK, even, odd)
     settle(owner_in.at[pl.ds(0, NA - 1)], ow_recv)
     land[e_here] = sketch[a]
 
@@ -212,34 +222,35 @@
             device_id_type=MESH,
         ).start()
 
-    settle(qv.at[0], q_recv.at[0])
-    queries_to(4, b_at[NB - 2], 1).start()
-    queries_to(5, b_at[NB - 2], 2).start()
-    settle(qv.at[0], q_recv.at[1])
-    queries_to(6, b_at[2], NB - 1).start()
-    settle(land.at[pl.ds(0, NA * LINE - 1)], s1_recv)
+    lanes = lax.broadcasted_iota(jnp.int32, (NA * LINE, 128), 1)
+    named = dp_of(lanes // NB, lanes % NB)
+    onehot = (owner_in[...].reshape(NA * LINE, 128) == named).astype(F32).astype(BF16)
     for step in range(2, NB - 1):
         settle(qv.at[0], q_recv.at[step])
-
-    total = jnp.zeros((NA * LINE, QS), F32)
-    for i in range(NB):
-        total += lax.dot_general(
-            land[:, i, :].astype(BF16), qv[i], NT, preferred_element_type=F32
-        )
+    settle(land.at[pl.ds(0, NA * LINE - 1)], s1_recv)
+
+    total = lax.dot_general(
+        jnp.concatenate([land[:, i, :] for i in range(NB)], axis=1).astype(BF16),
+        jnp.concatenate([qv[i] for i in range(NB)], axis=1),
+        NT,
+        preferred_element_type=F32,
+    )
     part[...] = total.reshape(NA, 8, QS)
-    lanes = lax.broadcasted_iota(jnp.int32, (NA * LINE, 128), 1)
-    named = dp_of(lanes // NB, lanes % NB)
-    onehot = (owner_in[...].reshape(NA * LINE, 128) == named).astype(F32)
+    high = total.astype(BF16)
+    rest = total - high.astype(F32)
+    mid = rest.astype(BF16)
+    low = (rest - mid.astype(F32)).astype(BF16)
     summed = lax.dot_general(
-        onehot, total, TN, precision=lax.Precision.HIGHEST, preferred_element_type=F32
+        jnp.concatenate([onehot] * 3, axis=0),
+        jnp.concatenate([high, mid, low], axis=0),
+        TN,
+        preferred_element_type=F32,
     )
     for i in range(NA):
         opart[i] = summed[i * NB : (i + 1) * NB]
-    part_in[a] = part[a]
-    opart_in[a] = opart[a]
-
-    for i in a_at[2:] + a_at[1:2]:
-        for src, dst, k in ((part, part_in, 0), (opart, opart_in, 1)):
+    for src, dst, k in ((opart, opart_in, 1), (part, part_in, 0)):
+        dst[a] = src[a]
+        for i in a_at[2:] + a_at[1:2]:
             pltpu.make_async_remote_copy(
                 src_ref=src.at[i],
                 dst_ref=dst.at[a],
@@ -249,15 +260,10 @@
                 device_id_type=MESH,
             ).start()
 
-    settle(part_in.at[pl.ds(0, NA - 1)], s2_recv.at[0])
     settle(opart_in.at[pl.ds(0, NA - 1)], s2_recv.at[1])
-    sc[...] = jnp.sum(part_in[...], axis=0)
     owned = jnp.sum(opart_in[...], axis=0)
     for i in range(NB):
         oo[i] = owned[i : i + 1]
-
-    sc_in[t] = sc[...]
-    oo_in[b * NT_DEV + t] = oo[b]
 
     def send_total(i, j):
         pltpu.make_async_remote_copy(
@@ -271,6 +277,8 @@
 
     for i, j in beyond:
         send_total(i, j)
+    settle(part_in.at[pl.ds(0, NA - 1)], s2_recv.at[0])
+    sc[...] = jnp.sum(part_in[...], axis=0)
     for i, j in column[len(beyond) :]:
         pltpu.make_async_remote_copy(
             src_ref=sc,
@@ -281,6 +289,8 @@
             device_id_type=MESH,
         ).start()
         send_total(i, j)
+    sc_in[t] = sc[...]
+    oo_in[b * NT_DEV + t] = oo[b]
     settle(sc_in.at[pl.ds(0, NT_DEV - 1)], s3_recv.at[0])
     for i in range(NT_DEV):
         scores_ref[:, i * QS : (i + 1) * QS] = sc_in[i]
@@ -304,7 +314,7 @@
 
 def shards(hidden_acts, out_grads, proj_in, proj_out, queries, owner):
     ff, d = hidden_acts.shape[1], out_grads.shape[1]
-    pieces = hidden_acts.shape[0] // CHUNK
+    blocks = hidden_acts.shape[0] // TOK
     entries = queries.shape[1]
     hbm = pl.BlockSpec(memory_space=pl.ANY)
     vmem = pl.BlockSpec(memory_space=pltpu.VMEM)
@@ -318,16 +328,16 @@
         in_specs=[hbm] * 6,
         out_specs=(vmem, vmem),
         scratch_shapes=[
-            pltpu.VMEM((pieces, CHUNK, ff), BF16),
-            pltpu.VMEM((pieces, CHUNK, d), BF16),
+            pltpu.VMEM((blocks, TOK, ff), BF16),
+            pltpu.VMEM((blocks, TOK, d), BF16),
             pltpu.VMEM((RANK, ff), BF16),
             pltpu.VMEM((RANK, d), BF16),
-            pltpu.VMEM((2, TOK, 2 * RANK), BF16),
-            pltpu.VMEM((TOK, 2 * RANK), F32),
-            pltpu.VMEM((TOK, 2 * RANK), F32),
-            pltpu.VMEM((2, TOK, 2 * RANK), BF16),
-            pltpu.VMEM((TOK, 2 * RANK), F32),
-            pltpu.VMEM((128, 128), F32),
+            pltpu.VMEM((2, 2 * RANK, TOK), BF16),
+            pltpu.VMEM((2 * RANK, TOK), F32),
+            pltpu.VMEM((2 * RANK, TOK), F32),
+            pltpu.VMEM((2, 2 * RANK, TOK), BF16),
+            pltpu.VMEM((2 * RANK, TOK), F32),
+            pltpu.VMEM((RANK, 2 * RANK), F32),
             pltpu.VMEM((NA, NB, 128), F32),
             pltpu.VMEM((NA * LINE, NB, 128), F32),
             pltpu.VMEM((NB, QS, entries), BF16),
@@ -342,7 +352,7 @@
             pltpu.VMEM((NB, 1, QS), F32),
             pltpu.VMEM((NT_DEV, 8, QS), F32),
             pltpu.VMEM((NB * NT_DEV, 1, QS), F32),
-            dma((2, pieces)),
+            dma((2, blocks)),
             dma((2,)),
             dma((2,)),
             dma((3,)),

time: 33.3 us -> 32.3 us (0.970)
  Pallas kernels: 30.7 us -> 29.7 us
    pallas_call x1, Pallas kernels: 30.7 us -> 29.7 us  [shards(): pl.pallas_call(kernel, out_shape=(jax.ShapeDtypeStruct((8, NT_DEV * QS),...]
where the time goes in v3:
time: 32.3 us; the launch traced here: 32.2 us
  Pallas kernels  29.7 us (92%)
  local copies, waits for them, and re-layouts  1.86 us (6%)
  between operations  0.65 us (2%)
    pallas_call x1, Pallas kernels, shards(): pl.pallas_call(kernel, out_shape=(jax.ShapeDtypeStruct((8, NT_DEV * QS),...  29.7 us
    unnamed x4, local copies, waits for them, and re-layouts  1.86 us

profile of v3, /device:TPU:1, one launch (start us, length us, event | category | flops | bytes accessed | tf_op | source)
XLA Modules:
  0.0 32.2 jit_solution(8103306261371655908)
XLA Ops:
  0.6 0.0 copy-start
  0.6 0.6 %copy-done = s32[8]{0:T(128)S(1)} copy-done((s32[8]{0:T(128)S(1)}, s32[8]{0:T(128)}, u32[]{:S(2)}) %copy-start) | copy-done | bytes 56
  1.3 29.7 %attribution.1 = (f32[8,1024]{1,0:T(8,128)S(1)}, f32[1,1024]{1,0:T(1,128)S(1)}) custom-call(bf16[1024,3584]{1,0:T(8,128)(2,1)} %h_ref.1, bf16[1024,1024]{1,0:T(8,128)(2,1)} %g_ref.1, bf16[64,3584]{1,0:T(8,128)(2,1)} %bitcast.2, bf16[64,1024]{1,0:T(8,128)(2,1)} %bitcast.3, bf16[1024,128]{1,0:T(8,128)(2,1)} %q_ref.1, s32[8]{0:T(128)S(1)} %copy-done), custom_call_target="tpu_custom_call" | custom-call | tf_op jit(solution)/shard_map/attribution/pallas_call | solution.py:322
  31.0 0.6 %copy.10 = f32[8,1024]{1,0:T(8,128)} copy(f32[8,1024]{1,0:T(8,128)S(1)} %get-tuple-element.4) | data formatting | bytes 65536
  31.6 0.6 %copy.11 = f32[1,1024]{1,0:T(1,128)} copy(f32[1,1024]{1,0:T(1,128)S(1)} %get-tuple-element.5) | data formatting | bytes 8192
Async XLA Ops:
  0.6 0.7 %copy-start = (s32[8]{0:T(128)S(1)}, s32[8]{0:T(128)}, u32[]{:S(2)}) copy-start(s32[8]{0:T(128)} %owner_ref.1) | copy-start | bytes 100

commit v4 on v3

--- a/solution.py
+++ b/solution.py
@@ -138,6 +138,8 @@
 
     def meet(ready):
         pl.semaphore_wait(barrier, len(greeted))
+        for step, j in enumerate((2, NB - 2, 1, NB - 1)):
+            queries_to(step, b, j).start()
         for copy in rs[:ready]:
             copy.start()
         for to in a_at[1:]:
@@ -149,12 +151,19 @@
                 device_id={"dp": dp_of(to, b)},
                 device_id_type=MESH,
             ).start()
-        for step, j in enumerate((2, NB - 2, 1, NB - 1)):
-            queries_to(step, b, j).start()
 
     early = b < 1
     for c in range(NT_DEV):
         if c == 0:
+            o_own.wait()
+            row = lax.broadcasted_iota(jnp.int32, (8, 128), 0)
+            tile = jnp.zeros((8, 128), jnp.int32)
+            for e in range(8):
+                tile = jnp.where(row == e, owner_s[e], tile)
+            owner_t[...] = tile
+            owner_in[a] = tile
+            q_own.wait()
+            pl.when(jnp.logical_not(early))(lambda: meet(0))
             w_in.wait()
             w_out.wait()
         for copy in loads[c]:
@@ -172,15 +181,7 @@
         else:
             own[...] = both
         if c == 0:
-            o_own.wait()
-            row = lax.broadcasted_iota(jnp.int32, (8, 128), 0)
-            tile = jnp.zeros((8, 128), jnp.int32)
-            for e in range(8):
-                tile = jnp.where(row == e, owner_s[e], tile)
-            owner_t[...] = tile
-            owner_in[a] = tile
-            q_own.wait()
-            pl.when(jnp.logical_not(early))(lambda: meet(1))
+            pl.when(jnp.logical_not(early))(rs[0].start)
         elif c < 3:
             pl.when(jnp.logical_not(early))(rs[c].start)
         else:
@@ -210,7 +211,6 @@
         odd = outer[pl.ds(2 * i * NB + 1, NB, stride=2), :]
         sketch[i] = jnp.where(lane < RANK, even, odd)
     settle(owner_in.at[pl.ds(0, NA - 1)], ow_recv)
-    land[e_here] = sketch[a]
 
     for i, j, k in plane:
         pltpu.make_async_remote_copy(
@@ -222,6 +222,7 @@
             device_id_type=MESH,
         ).start()
 
+    land[e_here] = sketch[a]
     lanes = lax.broadcasted_iota(jnp.int32, (NA * LINE, 128), 1)
     named = dp_of(lanes // NB, lanes % NB)
     onehot = (owner_in[...].reshape(NA * LINE, 128) == named).astype(F32).astype(BF16)
@@ -235,7 +236,6 @@
         NT,
         preferred_element_type=F32,
     )
-    part[...] = total.reshape(NA, 8, QS)
     high = total.astype(BF16)
     rest = total - high.astype(F32)
     mid = rest.astype(BF16)
@@ -249,7 +249,8 @@
     for i in range(NA):
         opart[i] = summed[i * NB : (i + 1) * NB]
     for src, dst, k in ((opart, opart_in, 1), (part, part_in, 0)):
-        dst[a] = src[a]
+        if src is part:
+            part[...] = total.reshape(NA, 8, QS)
         for i in a_at[2:] + a_at[1:2]:
             pltpu.make_async_remote_copy(
                 src_ref=src.at[i],
@@ -259,6 +260,9 @@
                 device_id={"dp": dp_of(i, b)},
                 device_id_type=MESH,
             ).start()
+
+    opart_in[a] = opart[a]
+    part_in[a] = part[a]
 
     settle(opart_in.at[pl.ds(0, NA - 1)], s2_recv.at[1])
     owned = jnp.sum(opart_in[...], axis=0)

time: 32.3 us -> 32.2 us (level)
  no operation moved by 1% of the time
where the time goes in v4:
time: 32.2 us; the launch traced here: 32.1 us
  Pallas kernels  29.6 us (92%)
  local copies, waits for them, and re-layouts  1.86 us (6%)
  between operations  0.65 us (2%)
    pallas_call x1, Pallas kernels, shards(): pl.pallas_call(kernel, out_shape=(jax.ShapeDtypeStruct((8, NT_DEV * QS),...  29.6 us
    unnamed x4, local copies, waits for them, and re-layouts  1.86 us

profile of v4, /device:TPU:1, one launch (start us, length us, event | category | flops | bytes accessed | tf_op | source)
XLA Modules:
  0.0 32.1 jit_solution(2385794391217912116)
XLA Ops:
  0.6 0.0 copy-start
  0.6 0.6 %copy-done = s32[8]{0:T(128)S(1)} copy-done((s32[8]{0:T(128)S(1)}, s32[8]{0:T(128)}, u32[]{:S(2)}) %copy-start) | copy-done | bytes 56
  1.3 29.6 %attribution.1 = (f32[8,1024]{1,0:T(8,128)S(1)}, f32[1,1024]{1,0:T(1,128)S(1)}) custom-call(bf16[1024,3584]{1,0:T(8,128)(2,1)} %h_ref.1, bf16[1024,1024]{1,0:T(8,128)(2,1)} %g_ref.1, bf16[64,3584]{1,0:T(8,128)(2,1)} %bitcast.2, bf16[64,1024]{1,0:T(8,128)(2,1)} %bitcast.3, bf16[1024,128]{1,0:T(8,128)(2,1)} %q_ref.1, s32[8]{0:T(128)S(1)} %copy-done), custom_call_target="tpu_custom_call" | custom-call | tf_op jit(solution)/shard_map/attribution/pallas_call | solution.py:326
  30.9 0.6 %copy.10 = f32[8,1024]{1,0:T(8,128)} copy(f32[8,1024]{1,0:T(8,128)S(1)} %get-tuple-element.4) | data formatting | bytes 65536
  31.6 0.6 %copy.11 = f32[1,1024]{1,0:T(1,128)} copy(f32[1,1024]{1,0:T(1,128)S(1)} %get-tuple-element.5) | data formatting | bytes 8192
Async XLA Ops:
  0.6 0.7 %copy-start = (s32[8]{0:T(128)S(1)}, s32[8]{0:T(128)}, u32[]{:S(2)}) copy-start(s32[8]{0:T(128)} %owner_ref.1) | copy-start | bytes 100
